TPU v7x, 256 devices: a whole 4x4x8 slice. The times are simulated.
256 devices in a mesh: grp: 16 (over y, x_hi, core), dom: 16 (over z, x_lo).
Axes of the slice: x: 4 (x_hi: 2, x_lo: 2; x = x_hi * 2 + x_lo), y: 4, z: 8, core: 2. Of those that a mesh axis runs over, the one named last changes fastest.
Arguments:
- queries: bfloat16 [65536, 256], P(('grp', 'dom')), may hold values from -6 to 6
- key_rows: bfloat16 [65536, 256], P(('grp', 'dom')), may hold values from -6 to 6
- value_rows: bfloat16 [65536, 256], P(('grp', 'dom')), may hold values from -6 to 6
- saved_output: bfloat16 [65536, 256], P(('grp', 'dom')), may hold values from -6 to 6
- output_grad: bfloat16 [65536, 256], P(('grp', 'dom')), may hold values from -24 to 24
- log_norm: float32 [8, 65536], P(None, ('grp', 'dom')), may hold values from 5 to 8
- local_lists: int32 [512, 32], P(('grp', 'dom')), may hold values from 0 to 31, as said below
- expander_lists: int32 [512, 16], P(('grp', 'dom')), may hold values from 0 to 31, as said below
- local_counts: int32 [512], P(('grp', 'dom')), may hold values from 1 to 32, as said below
- expander_counts: int32 [512], P(('grp', 'dom')), may hold values from 1 to 16, as said below
Outputs:
- query_grad: bfloat16 [65536, 256], P(('grp', 'dom'))
- key_grad: bfloat16 [65536, 256], P(('grp', 'dom'))
- value_grad: bfloat16 [65536, 256], P(('grp', 'dom'))
Inputs may be any that keep to these rules, and one draw needn't show every extreme that they name: `local_lists`: each row is an ordering of all 32 blocks of the partition. `expander_lists`: entries of a row are distinct and never name the block's own partition. `local_counts`: some block uses its whole list. `expander_counts`: some block uses its whole list.
All inputs are finite; a program needn't handle non-finite values.
Results may differ from a plain program's by a relative error of at most 0.0054.
Values may be sent and summed in bfloat16 or wider, within the bound.
A program may use at most 128 MiB of HBM per device.

v0:
```python
import math

import jax
import jax.numpy as jnp
from jax import lax
from jax.experimental import pallas as pl
from jax.experimental.pallas import tpu as pltpu
from jax.sharding import PartitionSpec as P

HEADS = 8
HEAD_DIM = 32
BLOCK = 128
ROWS = 256
D = 256
N_Z, N_Y = 8, 4
Q_SLOTS = 11
K_SLOTS = 5
META = 24
HIDE = 1e30
SCALING = 1.0 / math.sqrt(HEAD_DIM)
LOG2E = math.log2(math.e)
MESH = pl.DeviceIdType.MESH
ANY = pl.BlockSpec(memory_space=pl.ANY)
VMEM = pl.BlockSpec(memory_space=pltpu.VMEM)
SMEM = pl.BlockSpec(memory_space=pltpu.SMEM)
VMEM_LIMIT = 56 * 1024 * 1024
FAR, NEAR, ACROSS = 0, 1, 2
STEPS = (
    (0, NEAR), (0, FAR), (1, FAR), (7, FAR), (2, FAR), (6, FAR), (0, ACROSS), (8, ACROSS),
    (10, ACROSS), (3, FAR), (5, FAR), (4, FAR), (9, ACROSS), (9, NEAR), (8, NEAR), (10, NEAR),
)
KEY_SLOTS = {FAR: (0, 1), NEAR: (0, 2), ACROSS: (3, 4)}
NT = (((1,), (1,)), ((), ()))
NN = (((1,), (0,)), ((), ()))


def dot(a, b, dims):
    return lax.dot_general(a, b, dims, preferred_element_type=jnp.float32)


def places():
    g, m = lax.axis_index("grp"), lax.axis_index("dom")
    return g // 4, g // 2 % 2, g % 2, m // 2, m % 2


def partners(y, xh, c, z, xl):
    def at(y=y, xh=xh, c=c, z=z, xl=xl):
        return ((y * 2 + xh) * 2 + c, z * 2 + xl)

    return {
        "right": at(z=(z + 1) % N_Z),
        "left": at(z=(z + N_Z - 1) % N_Z),
        "right3": at(z=(z + 3) % N_Z),
        "left3": at(z=(z + N_Z - 3) % N_Z),
        "y1": at(y=(y + 1) % N_Y),
        "y2": at(y=(y + 2) % N_Y),
        "y3": at(y=(y + 3) % N_Y),
        "far_x": at(xh=1 - xh),
        "near_x": at(xl=1 - xl),
        "sibling": at(c=1 - c),
    }


def kernel(
    q_ref, g_ref, o_ref, k_ref, v_ref, lse_ref, ll_ref, el_ref, lc_ref, ec_ref,
    sums,
    qb, gb, ob, qt, gt, meta, kk, vv, km, vm, kt, dqa, dka, dva,
    ring_out, ring_in, y_out, y_in, x_out, x_in,
    in_sem, ring_send, ring_recv, y_send, y_recv, x_send, x_recv,
    rr_send, rr_recv, ry_send, ry_recv, rx_send, rx_recv,
):
    y, xh, c, z, xl = places()
    others = partners(y, xh, c, z, xl)
    f32, bf16 = jnp.float32, jnp.bfloat16

    def remote(src, dst, send, recv, who):
        return pltpu.make_async_remote_copy(
            src_ref=src, dst_ref=dst, send_sem=send, recv_sem=recv,
            device_id=others[who], device_id_type=MESH,
        )

    held = (qt, gt, meta)
    halves = ((0, BLOCK), (0, BLOCK), (0, 16))
    sizes = ((BLOCK, BLOCK), (BLOCK, BLOCK), (16, 8))

    def ring(hop, kind, way):
        whole = held[kind]
        src, dst = ((N_Z - hop) % N_Z, N_Z - 1 - hop) if way == 0 else (hop, hop + 1)
        src, dst = whole.at[src], whole.at[dst]
        if hop == 3:
            start = 0 if way == 0 else sizes[kind][0]
            rows = pl.ds(start, sizes[kind][way])
            src, dst = src.at[rows], dst.at[rows]
        return remote(
            src, dst, ring_send.at[hop, kind, way], ring_recv.at[hop, kind, way],
            "right" if way == 0 else "left",
        )

    def ycopy(step, kind):
        whole = held[kind]
        return remote(
            whole.at[0], whole.at[N_Z - 1 + N_Y - step], y_send.at[step - 1, kind],
            y_recv.at[step - 1, kind], f"y{step}",
        )

    def xcopy(what, i):
        whole, own = (kk, k_ref) if i == 0 else (vv, v_ref)
        number, who = {"near": (0, "near_x"), "sib": (1, "sibling"), "far": (2, "far_x"), "on": (3, "sibling")}[what]
        src = whole.at[3] if what == "on" else own
        return remote(src, whole.at[number + 1], x_send.at[number, i], x_recv.at[number, i], who)

    def ring_back(hop, way):
        buf, into = ring_out.at[hop, way], ring_in.at[hop, way]
        if hop == 0:
            rows = pl.ds(way * BLOCK, BLOCK)
            buf, into = buf.at[rows], into.at[rows]
        who = ("right", "left")[way] + ("3" if hop == 0 else "")
        return remote(buf, into, rr_send.at[hop, way], rr_recv.at[hop, way], who)

    def y_back(step, half=None):
        buf, into = y_out.at[step - 1], y_in.at[step - 1]
        if half is not None:
            rows = pl.ds(half * BLOCK, BLOCK)
            buf, into = buf.at[rows], into.at[rows]
        at = (step - 1, half or 0)
        return remote(buf, into, ry_send.at[at], ry_recv.at[at], f"y{step}")

    def x_back(what, i):
        number, who = {"near": (0, "near_x"), "sib": (1, "sibling"), "pass": (2, "sibling"), "far": (3, "far_x")}[what]
        return remote(x_out.at[number, i], x_in.at[number, i], rx_send.at[number, i], rx_recv.at[number, i], who)

    barrier = pltpu.get_barrier_semaphore()
    for device in others.values():
        pl.semaphore_signal(barrier, inc=1, device_id=device, device_id_type=MESH)
    loads = [
        pltpu.make_async_copy(src, dst, in_sem.at[i])
        for i, (src, dst) in enumerate(
            ((q_ref, qb), (g_ref, gb), (o_ref, ob), (k_ref, kk.at[0]), (v_ref, vv.at[0]))
        )
    ]
    for load in loads:
        load.start()

    lane = lax.broadcasted_iota(jnp.int32, (8, 128), 1)

    def mark(lists, counts, e, base):
        def one(s, hidden):
            hit = (lane == base + lists[e, s]) & (s < counts[e])
            return jnp.where(hit, 0.0, hidden)
        return one

    hidden = jnp.full((8, 128), HIDE, f32)
    for e in range(2):
        hidden = lax.fori_loop(0, ll_ref.shape[1], mark(ll_ref, lc_ref, e, e * 64), hidden)
        hidden = lax.fori_loop(0, el_ref.shape[1], mark(el_ref, ec_ref, e, e * 64 + 32), hidden)
    meta[0, 16:24, 0:128] = hidden
    meta[0, 16:24, 128:256] = hidden
    meta[0, 0:HEADS, :] = lse_ref[...] * LOG2E

    loads[0].wait()
    qt[0] = qb[...].astype(f32).T.astype(bf16)
    loads[1].wait()
    gt[0] = gb[...].astype(f32).T.astype(bf16)
    loads[2].wait()
    product = gb[...].astype(f32) * ob[...].astype(f32)
    high = product.astype(bf16)
    low = (product - high.astype(f32)).astype(bf16)
    rows_of = lax.broadcasted_iota(jnp.int32, (HEADS, D), 0)
    cols_of = lax.broadcasted_iota(jnp.int32, (HEADS, D), 1)
    pick = jnp.where(cols_of // HEAD_DIM == rows_of, 1.0, 0.0).astype(bf16)
    meta[0, HEADS:2 * HEADS, :] = dot(pick, high, NT) + dot(pick, low, NT)

    pl.semaphore_wait(barrier, len(others))
    for i in range(2):
        for what in ("near", "sib"):
            xcopy(what, i).start()
    for kind in range(3):
        for way in range(2):
            ring(0, kind, way).start()
        for step in (1, 3):
            ycopy(step, kind).start()
    for kind in range(3):
        ycopy(2, kind).start()

    dqa[...] = jnp.zeros_like(dqa)
    dka[...] = jnp.zeros_like(dka)
    dva[...] = jnp.zeros_like(dva)
    def spread(slot):
        kt[slot] = kk[slot].astype(f32).T.astype(bf16)
        for h in range(HEADS):
            cols = slice(h * HEAD_DIM, h * HEAD_DIM + HEAD_DIM)
            km[slot, h] = kk[slot, :, cols]
            vm[slot, h] = vv[slot, :, cols]

    def arrive(what):
        for i in range(2):
            xcopy(what, i).wait_recv()

    def pass_on(hop):
        for kind in range(3):
            for way in range(2):
                ring(hop - 1, kind, way).wait_recv()
                ring(hop, kind, way).start()

    def y_arrive(step):
        for kind in range(3):
            ycopy(step, kind).wait_recv()

    def send_back(hop, way):
        if hop == 0:
            rows = slice(way * BLOCK, way * BLOCK + BLOCK)
            ring_out[0, way, rows] = (dqa[4, rows] * SCALING).astype(bf16)
        else:
            total = dqa[4 - hop if way == 0 else 4 + hop] * SCALING
            if hop > 1:
                ring_back(hop - 1, way).wait_recv()
                total = total + ring_in[hop - 1, way].astype(f32)
            ring_out[hop, way] = total.astype(bf16)
        if hop == 3:
            rows = slice(way * BLOCK, way * BLOCK + BLOCK)
            rest = slice(BLOCK - way * BLOCK, ROWS - way * BLOCK)
            ring_back(0, way).wait_recv()
            ring_out[3, way, rows] = (total[rows] + ring_in[0, way, rows].astype(f32)).astype(bf16)
            ring_out[3, way, rest] = total[rest].astype(bf16)
        ring_back(hop, way).start()

    def y_send_back(step, half=None):
        rows = slice(None) if half is None else slice(half * BLOCK, half * BLOCK + BLOCK)
        y_out[step - 1, rows] = (dqa[N_Z - 1 + step, rows] * SCALING).astype(bf16)
        y_back(step, half).start()

    def x_send_back(what, number, slot):
        x_out[number, 0] = (dka[slot] * SCALING).astype(bf16)
        x_back(what, 0).start()
        x_out[number, 1] = dva[slot].astype(bf16)
        x_back(what, 1).start()

    def far_send_back():
        x_back("pass", 0).wait_recv()
        x_out[3, 0] = (dka[3] * SCALING + x_in[2, 0].astype(f32)).astype(bf16)
        x_back("far", 0).start()
        x_back("pass", 1).wait_recv()
        x_out[3, 1] = (dva[3] + x_in[2, 1].astype(f32)).astype(bf16)
        x_back("far", 1).start()

    def at_1():
        arrive("near")
        for i in range(2):
            xcopy("far", i).start()
        pass_on(1)
        spread(1)

    def at_4():
        pass_on(2)

    def at_5():
        arrive("far")
        for i in range(2):
            xcopy("on", i).start()
        spread(3)

    def at_6():
        arrive("on")
        spread(4)

    def at_7():
        y_arrive(3)

    def at_8():
        pass_on(3)
        y_arrive(1)

    def at_10():
        send_back(1, 0)

    def at_11():
        send_back(1, 1)
        for kind in range(3):
            for way in range(2):
                ring(3, kind, way).wait_recv()

    def at_12():
        x_send_back("near", 0, 1)
        send_back(0, 0)
        send_back(0, 1)
        y_arrive(2)

    def at_13():
        x_send_back("pass", 2, 4)
        send_back(2, 0)
        send_back(2, 1)

    def at_14():
        far_send_back()
        y_send_back(2)

    def at_15():
        y_send_back(1)
        send_back(3, 0)
        send_back(3, 1)

    events = {
        1: at_1, 4: at_4, 5: at_5, 6: at_6, 7: at_7, 8: at_8, 10: at_10, 11: at_11, 12: at_12,
        13: at_13, 14: at_14, 15: at_15,
    }

    spread_loads = loads[3:]
    for load in spread_loads:
        load.wait()
    spread(0)
    arrive("sib")
    spread(2)

    def table(s, values):
        if isinstance(s, int):
            return values[s]
        found = jnp.int32(values[0])
        for i, value in enumerate(values):
            if i > 0 and value != values[0]:
                found = jnp.where(s == i, jnp.int32(value), found)
        return found

    far_at = 32 + z * 4
    near_at = y * 8 + xh * 4
    across_at = y * 8 + (1 - xh) * 4
    one_lane = lax.broadcasted_iota(jnp.int32, (1, 128), 1)

    def step(s, carry):
        last = isinstance(s, int)
        for at, event in events.items():
            if not last:
                pl.when(s == at)(event)
            elif s == at:
                event()
        qd = table(s, [slot for slot, _ in STEPS])
        kind = table(s, [k for _, k in STEPS])
        key_slots = [table(s, [KEY_SLOTS[k][i] for _, k in STEPS]) for i in range(2)]
        start = near_at if last else jnp.where(kind == FAR, far_at, jnp.where(kind == NEAR, near_at, across_at))
        own = c if last else jnp.where(kind == FAR, xl, c)
        places_of = [start + own * 2, start + (1 - own) * 2]
        shown = meta[qd, 16:17, 0:128]
        hide = {}
        for i in range(2):
            for ke in range(2):
                cells = [
                    jnp.sum(jnp.where(one_lane == places_of[i] + (e * 64 + ke), shown, 0.0), axis=1, keepdims=True)
                    for e in range(2)
                ]
                hide[i, ke] = jnp.concatenate([jnp.broadcast_to(cell, (1, 128)) for cell in cells], axis=1)
        tiles = [(i, h) for h in range(HEADS) for i in range(2)]

        def first(tile):
            i, h = tile
            rows = slice(h * HEAD_DIM, h * HEAD_DIM + HEAD_DIM)
            return (
                dot(km[key_slots[i], h], qt[qd, rows, :], NN),
                dot(vm[key_slots[i], h], gt[qd, rows, :], NN),
            )

        def second(tile, scores, grad_p):
            i, h = tile
            lse, delta = meta[qd, h:h + 1, :], meta[qd, HEADS + h:HEADS + h + 1, :]
            low, grads = [], []
            for ke in range(2):
                rows = slice(ke * BLOCK, ke * BLOCK + BLOCK)
                attention = jnp.exp2(scores[rows] * (SCALING * LOG2E) - (lse + hide[i, ke]))
                low.append(attention.astype(bf16))
                grads.append((attention * (grad_p[rows] - delta)).astype(bf16))
            return jnp.concatenate(low, axis=0), jnp.concatenate(grads, axis=0)

        def third(tile, low, grads):
            i, h = tile
            rows = slice(h * HEAD_DIM, h * HEAD_DIM + HEAD_DIM)
            dva[key_slots[i], rows] += dot(gt[qd, rows, :], low, NT)
            dka[key_slots[i], rows] += dot(qt[qd, rows, :], grads, NT)
            dqa[qd, rows] += dot(kt[key_slots[i], rows, :], grads, NN)

        ones, twos = {}, {}
        for n in range(len(tiles) + 2):
            if n < len(tiles):
                ones[n] = first(tiles[n])
            if 0 <= n - 1 < len(tiles):
                twos[n - 1] = second(tiles[n - 1], *ones.pop(n - 1))
            if 0 <= n - 2 < len(tiles):
                third(tiles[n - 2], *twos.pop(n - 2))
            if last and n - 2 == len(tiles) // 2 - 1:
                y_send_back(3, 0)
        return carry

    lax.fori_loop(0, len(STEPS) - 1, step, 0)
    step(len(STEPS) - 1, 0)

    y_send_back(3, 1)
    x_send_back("sib", 1, 2)
    for i, own in enumerate((dka, dva)):
        total = own[0] * SCALING if i == 0 else own[0]
        for number, what in ((0, "near"), (1, "sib"), (3, "far")):
            x_back(what, i).wait_recv()
            total = total + x_in[number, i].astype(f32)
        sums[1 + i] = total.T.astype(bf16)
    total = dqa[0] * SCALING
    y_back(2).wait_recv()
    y_back(1).wait_recv()
    total = total + y_in[0].astype(f32) + y_in[1].astype(f32)
    for way in range(2):
        ring_back(3, way).wait_recv()
        total = total + ring_in[3, way].astype(f32)
    for half in range(2):
        y_back(3, half).wait_recv()
    total = total + y_in[2].astype(f32)
    sums[0] = total.astype(bf16)

    for hop in range(4):
        for way in range(2):
            for kind in range(3):
                ring(hop, kind, way).wait_send()
            ring_back(hop, way).wait_send()
    for s in (1, 2, 3):
        for kind in range(3):
            ycopy(s, kind).wait_send()
    y_back(1).wait_send()
    y_back(2).wait_send()
    for half in range(2):
        y_back(3, half).wait_send()
    for i in range(2):
        for what in ("near", "sib", "far", "on"):
            xcopy(what, i).wait_send()
        for what in ("near", "sib", "pass", "far"):
            x_back(what, i).wait_send()


def turn_kernel(sums, q_out, k_out, v_out):
    q_out[...] = sums[0].astype(jnp.float32).T.astype(jnp.bfloat16)
    k_out[...] = sums[1]
    v_out[...] = sums[2]


def body(
    queries, key_rows, value_rows, saved_output, output_grad, log_norm,
    local_lists, expander_lists, local_counts, expander_counts,
):
    bf16, f32 = jnp.bfloat16, jnp.float32
    dma = pltpu.SemaphoreType.DMA
    tile = (ROWS, D)
    sums = pl.pallas_call(
        kernel,
        name="backward",
        out_shape=jax.ShapeDtypeStruct((3, *tile), bf16),
        in_specs=[ANY] * 5 + [VMEM] + [SMEM] * 4,
        out_specs=VMEM,
        scratch_shapes=[
            pltpu.VMEM(tile, bf16), pltpu.VMEM(tile, bf16), pltpu.VMEM(tile, bf16),
            pltpu.VMEM((Q_SLOTS, *tile), bf16), pltpu.VMEM((Q_SLOTS, *tile), bf16),
            pltpu.VMEM((Q_SLOTS, META, ROWS), f32),
            pltpu.VMEM((K_SLOTS, *tile), bf16), pltpu.VMEM((K_SLOTS, *tile), bf16),
            pltpu.VMEM((K_SLOTS, HEADS, ROWS, HEAD_DIM), bf16), pltpu.VMEM((K_SLOTS, HEADS, ROWS, HEAD_DIM), bf16),
            pltpu.VMEM((K_SLOTS, *tile), bf16),
            pltpu.VMEM((Q_SLOTS, *tile), f32),
            pltpu.VMEM((K_SLOTS, *tile), f32), pltpu.VMEM((K_SLOTS, *tile), f32),
            pltpu.VMEM((4, 2, *tile), bf16), pltpu.VMEM((4, 2, *tile), bf16),
            pltpu.VMEM((3, *tile), bf16), pltpu.VMEM((3, *tile), bf16),
            pltpu.VMEM((4, 2, *tile), bf16), pltpu.VMEM((4, 2, *tile), bf16),
            dma((5,)),
            dma((4, 3, 2)), dma((4, 3, 2)), dma((3, 3)), dma((3, 3)), dma((4, 2)), dma((4, 2)),
            dma((4, 2)), dma((4, 2)), dma((3, 2)), dma((3, 2)), dma((4, 2)), dma((4, 2)),
        ],
        compiler_params=pltpu.CompilerParams(
            collective_id=0, has_side_effects=True, vmem_limit_bytes=VMEM_LIMIT
        ),
    )(
        queries, output_grad, saved_output, key_rows, value_rows, log_norm,
        local_lists, expander_lists, local_counts, expander_counts,
    )
    return tuple(pl.pallas_call(
        turn_kernel,
        name="turn",
        out_shape=[jax.ShapeDtypeStruct(tile, bf16)] * 3,
        in_specs=[VMEM],
        out_specs=[VMEM] * 3,
    )(sums))


def solution(mesh):
    rows = P(("grp", "dom"), None)
    flat = P(("grp", "dom"))
    return jax.shard_map(
        body,
        mesh=mesh,
        in_specs=(rows, rows, rows, rows, rows, P(None, ("grp", "dom")), rows, rows, flat, flat),
        out_specs=(rows, rows, rows),
        check_vma=False,
    )
```

profile of v0, /device:TPU:4, one launch (start us, length us, event | category | flops | bytes accessed | tf_op | source)
XLA Modules:
  0.0 60.3 jit_solution(4616731092774470477)
XLA Ops:
  0.6 57.8 %backward.1.sums = bf16[3,256,256]{2,1,0:T(8,128)(2,1)} custom-call(bf16[256,256]{1,0:T(8,128)(2,1)} %q_ref.1, bf16[256,256]{1,0:T(8,128)(2,1)} %g_ref.1, bf16[256,256]{1,0:T(8,128)(2,1)} %o_ref.1, bf16[256,256]{1,0:T(8,128)(2,1)} %k_ref.1, bf16[256,256]{1,0:T(8,128)(2,1)} %v_ref.1, f32[8,256]{1,0:T(8,128)} %lse_ref.1, s32[2,32]{1,0:T(2,128)} %ll_ref.1, ...), custom_call_target="tpu_custom_call" | custom-call | tf_op jit(solution)/shard_map/backward/pallas_call | solution.py:445
  58.5 1.8 %turn.1 = (bf16[256,256]{1,0:T(8,128)(2,1)}, bf16[256,256]{1,0:T(8,128)(2,1)}, bf16[256,256]{1,0:T(8,128)(2,1)}) custom-call(bf16[3,256,256]{2,1,0:T(8,128)(2,1)} %backward.1.sums), custom_call_target="tpu_custom_call" | custom-call | tf_op jit(solution)/shard_map/turn/pallas_call | solution.py:474
where the time goes:
time: 60.4 us; the launch traced here: 60.3 us
  Pallas kernels  59.6 us (99%)
  between operations  0.64 us (1%)
    pallas_call x1, Pallas kernels, body(): pl.pallas_call(kernel, name='backward', out_shape=jax.ShapeDtypeStruct((3...  57.8 us
    pallas_call x1, Pallas kernels, body(): pl.pallas_call(turn_kernel, name='turn', out_shape=[jax.ShapeDtypeStruct(...  1.76 us

commit v1 on v0

--- a/solution.py
+++ b/solution.py
@@ -62,8 +62,9 @@
 
 
 def kernel(
-    q_ref, g_ref, o_ref, k_ref, v_ref, lse_ref, ll_ref, el_ref, lc_ref, ec_ref,
+    q_ref, g_ref, o_ref, k_ref, v_ref, lse_hbm, ll_hbm, el_hbm, lc_ref, ec_ref,
     sums,
+    lse_ref, ll_ref, el_ref,
     qb, gb, ob, qt, gt, meta, kk, vv, km, vm, kt, dqa, dka, dva,
     ring_out, ring_in, y_out, y_in, x_out, x_in,
     in_sem, ring_send, ring_recv, y_send, y_recv, x_send, x_recv,
@@ -135,7 +136,10 @@
     loads = [
         pltpu.make_async_copy(src, dst, in_sem.at[i])
         for i, (src, dst) in enumerate(
-            ((q_ref, qb), (g_ref, gb), (o_ref, ob), (k_ref, kk.at[0]), (v_ref, vv.at[0]))
+            (
+                (q_ref, qb), (g_ref, gb), (o_ref, ob), (k_ref, kk.at[0]), (v_ref, vv.at[0]),
+                (lse_hbm, lse_ref), (ll_hbm, ll_ref), (el_hbm, el_ref),
+            )
         )
     ]
     for load in loads:
@@ -149,6 +153,8 @@
             return jnp.where(hit, 0.0, hidden)
         return one
 
+    for load in loads[5:]:
+        load.wait()
     hidden = jnp.full((8, 128), HIDE, f32)
     for e in range(2):
         hidden = lax.fori_loop(0, ll_ref.shape[1], mark(ll_ref, lc_ref, e, e * 64), hidden)
@@ -304,7 +310,7 @@
         13: at_13, 14: at_14, 15: at_15,
     }
 
-    spread_loads = loads[3:]
+    spread_loads = loads[3:5]
     for load in spread_loads:
         load.wait()
     spread(0)
@@ -446,9 +452,11 @@
         kernel,
         name="backward",
         out_shape=jax.ShapeDtypeStruct((3, *tile), bf16),
-        in_specs=[ANY] * 5 + [VMEM] + [SMEM] * 4,
+        in_specs=[ANY] * 8 + [SMEM] * 2,
         out_specs=VMEM,
         scratch_shapes=[
+            pltpu.VMEM(log_norm.shape, f32), pltpu.SMEM(local_lists.shape, jnp.int32),
+            pltpu.SMEM(expander_lists.shape, jnp.int32),
             pltpu.VMEM(tile, bf16), pltpu.VMEM(tile, bf16), pltpu.VMEM(tile, bf16),
             pltpu.VMEM((Q_SLOTS, *tile), bf16), pltpu.VMEM((Q_SLOTS, *tile), bf16),
             pltpu.VMEM((Q_SLOTS, META, ROWS), f32),
@@ -460,7 +468,7 @@
             pltpu.VMEM((4, 2, *tile), bf16), pltpu.VMEM((4, 2, *tile), bf16),
             pltpu.VMEM((3, *tile), bf16), pltpu.VMEM((3, *tile), bf16),
             pltpu.VMEM((4, 2, *tile), bf16), pltpu.VMEM((4, 2, *tile), bf16),
-            dma((5,)),
+            dma((8,)),
             dma((4, 3, 2)), dma((4, 3, 2)), dma((3, 3)), dma((3, 3)), dma((4, 2)), dma((4, 2)),
             dma((4, 2)), dma((4, 2)), dma((3, 2)), dma((3, 2)), dma((4, 2)), dma((4, 2)),
         ],

time: 60.4 us -> 60.1 us (level)
  no operation moved by 1% of the time
where the time goes in v1:
time: 60.1 us; the launch traced here: 59.9 us
  Pallas kernels  59.3 us (99%)
  between operations  0.64 us (1%)
    pallas_call x1, Pallas kernels, body(): pl.pallas_call(kernel, name='backward', out_shape=jax.ShapeDtypeStruct((3...  57.5 us
    pallas_call x1, Pallas kernels, body(): pl.pallas_call(turn_kernel, name='turn', out_shape=[jax.ShapeDtypeStruct(...  1.76 us

profile of v1, /device:TPU:4, one launch (start us, length us, event | category | flops | bytes accessed | tf_op | source)
XLA Modules:
  0.0 59.9 jit_solution(16349371677925302778)
XLA Ops:
  0.6 57.5 %backward.1.sums = bf16[3,256,256]{2,1,0:T(8,128)(2,1)} custom-call(bf16[256,256]{1,0:T(8,128)(2,1)} %q_ref.1, bf16[256,256]{1,0:T(8,128)(2,1)} %g_ref.1, bf16[256,256]{1,0:T(8,128)(2,1)} %o_ref.1, bf16[256,256]{1,0:T(8,128)(2,1)} %k_ref.1, bf16[256,256]{1,0:T(8,128)(2,1)} %v_ref.1, f32[8,256]{1,0:T(8,128)} %lse_hbm.1, s32[2,32]{1,0:T(2,128)} %ll_hbm.1, ...), custom_call_target="tpu_custom_call" | custom-call | tf_op jit(solution)/shard_map/backward/pallas_call | solution.py:451
  58.1 1.8 %turn.1 = (bf16[256,256]{1,0:T(8,128)(2,1)}, bf16[256,256]{1,0:T(8,128)(2,1)}, bf16[256,256]{1,0:T(8,128)(2,1)}) custom-call(bf16[3,256,256]{2,1,0:T(8,128)(2,1)} %backward.1.sums), custom_call_target="tpu_custom_call" | custom-call | tf_op jit(solution)/shard_map/turn/pallas_call | solution.py:482

commit v2 on v1

--- a/solution.py
+++ b/solution.py
@@ -62,9 +62,9 @@
 
 
 def kernel(
-    q_ref, g_ref, o_ref, k_ref, v_ref, lse_hbm, ll_hbm, el_hbm, lc_ref, ec_ref,
+    q_ref, g_ref, o_ref, k_ref, v_ref, lse_hbm, ll_hbm, el_hbm, lc_hbm, ec_hbm,
     sums,
-    lse_ref, ll_ref, el_ref,
+    lse_ref, ll_ref, el_ref, lc_ref, ec_ref,
     qb, gb, ob, qt, gt, meta, kk, vv, km, vm, kt, dqa, dka, dva,
     ring_out, ring_in, y_out, y_in, x_out, x_in,
     in_sem, ring_send, ring_recv, y_send, y_recv, x_send, x_recv,
@@ -139,6 +139,7 @@
             (
                 (q_ref, qb), (g_ref, gb), (o_ref, ob), (k_ref, kk.at[0]), (v_ref, vv.at[0]),
                 (lse_hbm, lse_ref), (ll_hbm, ll_ref), (el_hbm, el_ref),
+                (lc_hbm, lc_ref), (ec_hbm, ec_ref),
             )
         )
     ]
@@ -452,11 +453,12 @@
         kernel,
         name="backward",
         out_shape=jax.ShapeDtypeStruct((3, *tile), bf16),
-        in_specs=[ANY] * 8 + [SMEM] * 2,
+        in_specs=[ANY] * 10,
         out_specs=VMEM,
         scratch_shapes=[
             pltpu.VMEM(log_norm.shape, f32), pltpu.SMEM(local_lists.shape, jnp.int32),
             pltpu.SMEM(expander_lists.shape, jnp.int32),
+            pltpu.SMEM(local_counts.shape, jnp.int32), pltpu.SMEM(expander_counts.shape, jnp.int32),
             pltpu.VMEM(tile, bf16), pltpu.VMEM(tile, bf16), pltpu.VMEM(tile, bf16),
             pltpu.VMEM((Q_SLOTS, *tile), bf16), pltpu.VMEM((Q_SLOTS, *tile), bf16),
             pltpu.VMEM((Q_SLOTS, META, ROWS), f32),
@@ -468,7 +470,7 @@
             pltpu.VMEM((4, 2, *tile), bf16), pltpu.VMEM((4, 2, *tile), bf16),
             pltpu.VMEM((3, *tile), bf16), pltpu.VMEM((3, *tile), bf16),
             pltpu.VMEM((4, 2, *tile), bf16), pltpu.VMEM((4, 2, *tile), bf16),
-            dma((8,)),
+            dma((10,)),
             dma((4, 3, 2)), dma((4, 3, 2)), dma((3, 3)), dma((3, 3)), dma((4, 2)), dma((4, 2)),
             dma((4, 2)), dma((4, 2)), dma((3, 2)), dma((3, 2)), dma((4, 2)), dma((4, 2)),
         ],

time: 60.1 us -> 59.4 us (0.988)
  Pallas kernels: 59.3 us -> 58.6 us
    pallas_call x1, Pallas kernels: 57.5 us -> 56.9 us  [body(): pl.pallas_call(kernel, name='backward', out_shape=jax.ShapeDtypeStruct((3...]
where the time goes in v2:
time: 59.4 us; the launch traced here: 59.3 us
  Pallas kernels  58.6 us (99%)
  between operations  0.64 us (1%)
    pallas_call x1, Pallas kernels, body(): pl.pallas_call(kernel, name='backward', out_shape=jax.ShapeDtypeStruct((3...  56.9 us
    pallas_call x1, Pallas kernels, body(): pl.pallas_call(turn_kernel, name='turn', out_shape=[jax.ShapeDtypeStruct(...  1.76 us

profile of v2, /device:TPU:4, one launch (start us, length us, event | category | flops | bytes accessed | tf_op | source)
XLA Modules:
  0.0 59.3 jit_solution(9325597322217483838)
XLA Ops:
  0.6 56.9 %backward.1.sums = bf16[3,256,256]{2,1,0:T(8,128)(2,1)} custom-call(bf16[256,256]{1,0:T(8,128)(2,1)} %q_ref.1, bf16[256,256]{1,0:T(8,128)(2,1)} %g_ref.1, bf16[256,256]{1,0:T(8,128)(2,1)} %o_ref.1, bf16[256,256]{1,0:T(8,128)(2,1)} %k_ref.1, bf16[256,256]{1,0:T(8,128)(2,1)} %v_ref.1, f32[8,256]{1,0:T(8,128)} %lse_hbm.1, s32[2,32]{1,0:T(2,128)} %ll_hbm.1, ...), custom_call_target="tpu_custom_call" | custom-call | tf_op jit(solution)/shard_map/backward/pallas_call | solution.py:452
  57.5 1.8 %turn.1 = (bf16[256,256]{1,0:T(8,128)(2,1)}, bf16[256,256]{1,0:T(8,128)(2,1)}, bf16[256,256]{1,0:T(8,128)(2,1)}) custom-call(bf16[3,256,256]{2,1,0:T(8,128)(2,1)} %backward.1.sums), custom_call_target="tpu_custom_call" | custom-call | tf_op jit(solution)/shard_map/turn/pallas_call | solution.py:484
